TPU v7x, 256 devices: a whole 4x4x8 slice. The times are simulated.
256 devices in a mesh: dp: 16 (over y, z_lo), factor: 16 (over z_hi, x, core).
Axes of the slice: x: 4, y: 4, z: 8 (z_hi: 2, z_lo: 4; z = z_hi * 4 + z_lo), core: 2. Of those that a mesh axis runs over, the one named last changes fastest.
Arguments:
- inputs: bfloat16 [16384, 8192], P('dp', 'factor'), may hold values from -6 to 6
- cotangent: bfloat16 [16384, 8192], P('dp', 'factor'), may hold values from -6 to 6
- first_factor: bfloat16 [64, 128, 128], P('factor'), may hold values from -0.5 to 0.5
- second_factor: bfloat16 [64, 128, 512], P('factor'), may hold values from -0.5 to 0.5
- third_factor: bfloat16 [64, 512, 128], P('factor'), may hold values from -0.25 to 0.25
- fourth_factor: bfloat16 [64, 128, 128], P('factor'), may hold values from -0.5 to 0.5
Outputs:
- result: bfloat16 [16384, 8192], P('dp', 'factor')
- input_grad: bfloat16 [16384, 8192], P('dp', 'factor')
- first_grad: float32 [64, 128, 128], P('factor', 'dp')
- second_grad: float32 [64, 128, 512], P('factor', 'dp')
- third_grad: float32 [64, 512, 128], P('factor', 'dp')
- fourth_grad: float32 [64, 128, 128], P('factor', 'dp')
All inputs are finite; a program needn't handle non-finite values.
Results may differ from a plain program's by a relative error of at most 0.0069.
Values may be sent and summed in bfloat16 or wider, within the bound.
A program may use at most 64 MiB of HBM per device.

v0:
```python
import jax
import jax.numpy as jnp
from jax import lax
from jax.sharding import PartitionSpec as P


def gelu_tanh(values):
    return jax.nn.gelu(values, approximate=True)


def own_rows(values, position, members):
    rows = values.shape[1] // members
    return lax.dynamic_slice_in_dim(values, position * rows, rows, 1)


def local(inputs, cotangent, first_factor, second_factor, third_factor, fourth_factor):
    groups = lax.axis_size("factor")
    local_blocks = first_factor.shape[0]
    width_block = first_factor.shape[1]
    hidden_block = second_factor.shape[2]
    count = inputs.shape[0]
    blocks = local_blocks * groups
    stride = width_block // blocks
    tokens_in = inputs.reshape(count, local_blocks, width_block)
    grad_out = cotangent.reshape(count, local_blocks, width_block)
    second_view = second_factor.reshape(local_blocks, stride, blocks, hidden_block)
    fourth_view = fourth_factor.reshape(local_blocks, stride, blocks, width_block)
    first_out = jnp.einsum(
        "tbi,bik->bkt", tokens_in, first_factor, preferred_element_type=jnp.float32
    ).astype(jnp.bfloat16)
    grad_sent = jnp.einsum(
        "tco,crbo->crbt", grad_out, fourth_view, preferred_element_type=jnp.float32
    ).astype(jnp.bfloat16)
    grad_sent = grad_sent.reshape(local_blocks * stride, blocks, count)
    first_mixed = lax.all_to_all(first_out, "factor", split_axis=1, concat_axis=0, tiled=True)
    first_view = first_mixed.reshape(blocks, local_blocks, stride, count)
    pre_act = jnp.einsum(
        "bcrt,crbo->tco", first_view, second_view, preferred_element_type=jnp.float32
    )
    hidden = gelu_tanh(pre_act).astype(jnp.bfloat16)
    third_out = jnp.einsum(
        "tbh,bhk->bkt", hidden, third_factor, preferred_element_type=jnp.float32
    ).astype(jnp.bfloat16)
    third_mixed = lax.all_to_all(third_out, "factor", split_axis=1, concat_axis=0, tiled=True)
    third_view = third_mixed.reshape(blocks, local_blocks, stride, count)
    result = jnp.einsum(
        "bcrt,crbo->tco", third_view, fourth_view, preferred_element_type=jnp.float32
    ).astype(jnp.bfloat16)
    result = result.reshape(count, local_blocks * width_block)
    back_two = lax.all_to_all(grad_sent, "factor", split_axis=1, concat_axis=0, tiled=True)
    fourth_grad = jnp.einsum(
        "bcrt,tco->crbo", third_view, grad_out, preferred_element_type=jnp.float32
    )
    fourth_grad = fourth_grad.reshape(local_blocks, width_block, width_block)
    third_grad = jnp.einsum("tbh,kbt->bhk", hidden, back_two, preferred_element_type=jnp.float32)
    grad_hidden = jnp.einsum(
        "kbt,bhk->tbh", back_two, third_factor, preferred_element_type=jnp.float32
    )
    grad_pre = jax.vjp(gelu_tanh, pre_act)[1](grad_hidden)[0].astype(jnp.bfloat16)
    second_grad = jnp.einsum(
        "bcrt,tco->crbo", first_view, grad_pre, preferred_element_type=jnp.float32
    )
    second_grad = second_grad.reshape(local_blocks, width_block, hidden_block)
    first_sent = jnp.einsum(
        "tco,crbo->crbt", grad_pre, second_view, preferred_element_type=jnp.float32
    ).astype(jnp.bfloat16)
    first_sent = first_sent.reshape(local_blocks * stride, blocks, count)
    back_one = lax.all_to_all(first_sent, "factor", split_axis=1, concat_axis=0, tiled=True)
    first_grad = jnp.einsum("tbi,kbt->bik", tokens_in, back_one, preferred_element_type=jnp.float32)
    input_grad = jnp.einsum(
        "kbt,bik->tbi", back_one, first_factor, preferred_element_type=jnp.float32
    ).astype(jnp.bfloat16)
    input_grad = input_grad.reshape(count, local_blocks * width_block)
    first_grad, second_grad, third_grad, fourth_grad = lax.psum(
        (first_grad, second_grad, third_grad, fourth_grad), "dp"
    )
    members = lax.axis_size("dp")
    position = lax.axis_index("dp")
    first_grad = own_rows(first_grad, position, members)
    second_grad = own_rows(second_grad, position, members)
    third_grad = own_rows(third_grad, position, members)
    fourth_grad = own_rows(fourth_grad, position, members)
    return (result, input_grad, first_grad, second_grad, third_grad, fourth_grad)


def solution(mesh):
    in_specs = (
        P("dp", "factor"),
        P("dp", "factor"),
        P("factor", None, None),
        P("factor", None, None),
        P("factor", None, None),
        P("factor", None, None),
    )
    out_specs = (
        P("dp", "factor"),
        P("dp", "factor"),
        P("factor", "dp", None),
        P("factor", "dp", None),
        P("factor", "dp", None),
        P("factor", "dp", None),
    )
    return jax.shard_map(local, mesh=mesh, in_specs=in_specs, out_specs=out_specs, check_vma=False)
```

profile of v0, /device:TPU:2, one launch (start us, length us, event | category | flops | bytes accessed | tf_op | source)
XLA Modules:
  0.0 365.9 jit_solution(17556483839502437138)
XLA Ops:
  7.2 0.0 copy-start
  7.2 0.0 copy-start.4
  7.2 1.2 copy-done
  8.4 1.4 convolution_convert_fusion.3
  9.8 1.8 copy.58
  11.6 11.5 %all-to-all-start = ((bf16[4,128,1024]{2,0,1:T(4,128)(2,1)}), bf16[4,128,1024]{2,0,1:T(4,128)(2,1)S(1)}, u32[]{:S(2)}, u32[]{:S(2)}) async-start(bf16[4,128,1024]{2,0,1:T(4,128)(2,1)} %copy.58), calls=%async_computation | async-start | bytes 2097152 | tf_op jit(solution)/shard_map/all_to_all | solution.py:35
  23.0 1.3 reshape.56
  24.4 0.0 copy-done.4
  24.4 0.4 convolution_convert_fusion.1
  24.9 1.5 copy.64
  26.4 14.0 %all-to-all-done = bf16[4,128,1024]{2,0,1:T(4,128)(2,1)S(1)} async-done(((bf16[4,128,1024]{2,0,1:T(4,128)(2,1)}), bf16[4,128,1024]{2,0,1:T(4,128)(2,1)S(1)}, u32[]{:S(2)}, u32[]{:S(2)}) %all-to-all-start) | async-done | bytes 1048608 | tf_op jit(solution)/shard_map/all_to_all | solution.py:35
  40.4 14.8 %all-to-all-start.2 = ((bf16[8,64,1024]{2,0,1:T(8,128)(2,1)}), bf16[8,64,1024]{2,0,1:T(8,128)(2,1)}, u32[]{:S(2)}, u32[]{:S(2)}) async-start(bf16[8,64,1024]{2,0,1:T(8,128)(2,1)} %copy.64), calls=%async_computation.2 | async-start | bytes 2097152 | tf_op jit(solution)/shard_map/all_to_all | solution.py:50
  55.2 1.4 copy.119
  56.6 1.3 reshape.51
  57.9 0.0 copy-start.2
  58.0 7.6 %fusion.10 = (bf16[1024,4,512]{2,0,1:T(8,128)(2,1)}, f32[4,1024,512,1]{2,1,3,0:T(8,128)}) fusion(bf16[64,4,2,1024]{3,0,2,1:T(8,128)(2,1)S(1)} %reshape.51, bf16[4,2,64,512]{3,2,1,0:T(8,128)(2,1)} %bitcast.134), kind=kOutput, calls=%fused_computation.15 | convolution fusion | flops 555745280 | bytes 14155776 | tf_op jit(solution)/shard_map/bcrt,crbo->tco/dot_general | solution.py:37
  65.5 0.0 copy-done.2
  65.5 5.8 %all-to-all-done.2 = bf16[8,64,1024]{2,0,1:T(8,128)(2,1)} async-done(((bf16[8,64,1024]{2,0,1:T(8,128)(2,1)}), bf16[8,64,1024]{2,0,1:T(8,128)(2,1)}, u32[]{:S(2)}, u32[]{:S(2)}) %all-to-all-start.2) | async-done | bytes 1048608 | tf_op jit(solution)/shard_map/all_to_all | solution.py:50
  71.3 0.0 copy-start.5
  71.3 8.9 %fusion.6 = bf16[1024,4,512]{2,0,1:T(8,128)(2,1)S(1)} fusion(f32[4,1024,512,1]{2,1,3,0:T(8,128)} %get-tuple-element.35, bf16[4,512,128]{2,1,0:T(8,128)(2,1)} %param.10, bf16[16,8,4,1024]{3,1,2,0:T(8,128)(2,1)} %bitcast.18), kind=kOutput, calls=%fused_computation.8 | convolution fusion | flops 578813952 | bytes 14155776 | tf_op jit(solution)/shard_map/kbt,bhk->tbh/dot_general | solution.py:56
  80.2 0.0 copy-start.1
  80.2 2.0 copy-done.1
  82.2 0.0 copy-done.5
  82.2 1.5 fusion.15
  83.7 1.6 copy.67
  85.2 17.0 %all-to-all-start.3 = ((bf16[8,64,1024]{2,0,1:T(8,128)(2,1)}), bf16[8,64,1024]{2,0,1:T(8,128)(2,1)S(1)}, u32[]{:S(2)}, u32[]{:S(2)}) async-start(bf16[8,64,1024]{2,0,1:T(8,128)(2,1)} %copy.67), calls=%async_computation.3 | async-start | bytes 2097152 | tf_op jit(solution)/shard_map/all_to_all | solution.py:68
  102.2 4.5 %fusion.18 = bf16[4,128,1024]{1,2,0:T(8,128)(2,1)} fusion(bf16[1024,4,512]{2,0,1:T(8,128)(2,1)} %get-tuple-element.34, bf16[4,512,128]{2,1,0:T(8,128)(2,1)} %param.10), kind=kOutput, calls=%fused_computation.26 | convolution fusion | flops 537395200 | bytes 5767168 | tf_op jit(solution)/shard_map/tbh,bhk->bkt/dot_general | solution.py:41
  106.8 2.6 copy.60
  109.4 8.8 %all-to-all-done.3 = bf16[8,64,1024]{2,0,1:T(8,128)(2,1)S(1)} async-done(((bf16[8,64,1024]{2,0,1:T(8,128)(2,1)}), bf16[8,64,1024]{2,0,1:T(8,128)(2,1)S(1)}, u32[]{:S(2)}, u32[]{:S(2)}) %all-to-all-start.3) | async-done | bytes 1048608 | tf_op jit(solution)/shard_map/all_to_all | solution.py:68
  118.2 17.0 %all-to-all-start.1 = ((bf16[4,128,1024]{2,0,1:T(4,128)(2,1)}), bf16[4,128,1024]{2,0,1:T(4,128)(2,1)}, u32[]{:S(2)}, u32[]{:S(2)}) async-start(bf16[4,128,1024]{2,0,1:T(4,128)(2,1)} %copy.60), calls=%async_computation.1 | async-start | bytes 2097152 | tf_op jit(solution)/shard_map/all_to_all | solution.py:44
  135.2 0.2 all-reduce.3.cloned.1.call-start
  135.5 4.2 %fusion.11 = f32[4,512,64,2]{1,2,3,0:T(8,128)} fusion(bf16[64,4,2,1024]{3,0,2,1:T(8,128)(2,1)} %copy-done.2, bf16[1024,4,512]{2,0,1:T(8,128)(2,1)} %copy-done.1), kind=kOutput, calls=%fused_computation.16 | convolution fusion | flops 536870912 | bytes 6291456 | tf_op jit(solution)/shard_map/bcrt,tco->crbo/dot_general | solution.py:60
  139.7 5.1 %fusion.23 = f32[4,512,128]{2,1,0:T(8,128)} fusion(bf16[1024,4,512]{2,0,1:T(8,128)(2,1)} %get-tuple-element.34, bf16[16,8,4,1024]{3,1,2,0:T(8,128)(2,1)} %bitcast.18), kind=kOutput, calls=%fused_computation.32 | convolution fusion | flops 536870912 | bytes 6291456 | tf_op jit(solution)/shard_map/tbh,kbt->bhk/dot_general | solution.py:55
  144.7 0.0 copy-start.3
  144.7 1.1 convolution_bitcast_fusion
  145.9 5.5 %all-to-all-done.1 = bf16[4,128,1024]{2,0,1:T(4,128)(2,1)} async-done(((bf16[4,128,1024]{2,0,1:T(4,128)(2,1)}), bf16[4,128,1024]{2,0,1:T(4,128)(2,1)}, u32[]{:S(2)}, u32[]{:S(2)}) %all-to-all-start.1) | async-done | bytes 1048608 | tf_op jit(solution)/shard_map/all_to_all | solution.py:44
  151.4 1.5 copy.118
  152.9 1.8 copy.62
  154.7 2.1 reshape.53
  156.8 2.4 fusion.28
  159.2 0.0 all-reduce.3.cloned.1.call-update
  159.2 0.0 copy-done.3
  159.2 0.4 convolution_convert_fusion
  159.7 1.3 copy.73
  161.0 1.7 bitcast_convert_fusion
  162.7 1.3 copy.72
  164.0 189.0 %all-reduce.3.cloned.1.call-done = (f32[4,128,128]{1,2,0:T(8,128)}, f32[4,128,512]{2,1,0:T(8,128)}, f32[4,512,128]{2,1,0:T(8,128)}, f32[4,128,128]{2,1,0:T(8,128)}) async-done(((f32[4,128,128]{1,2,0:T(8,128)}, f32[4,128,512]{2,1,0:T(8,128)}, f32[4,512,128]{2,1,0:T(8,128)}, f32[4,128,128]{2,1,0:T(8,128)}), (f32[4,128,128]{1,2,0:T(8,128)}, f32[4,128,512]{2,1,0:T(8,128)}, f32[4,512,128]{2,1,0:T(8,128)}, ...) | async-done | bytes 2621456 | tf_op jit(solution)/shard_map/psum | solution.py:74
  353.0 1.1 constant_dynamic-slice_fusion.3
  354.1 0.7 copy.74
  354.8 1.5 constant_dynamic-slice_fusion.2
  356.3 1.3 constant_dynamic-slice_fusion
  357.6 1.5 constant_dynamic-slice_fusion.1
Async XLA Ops:
  7.2 1.2 copy-start
  7.2 17.2 %copy-start.4 = (bf16[4,128,128]{2,1,0:T(8,128)(2,1)S(1)}, bf16[4,128,128]{2,1,0:T(8,128)(2,1)}, u32[]{:S(2)}) copy-start(bf16[4,128,128]{2,1,0:T(8,128)(2,1)} %param.11) | copy-start | bytes 393220
  11.6 28.8 %all-to-all-start = ((bf16[4,128,1024]{2,0,1:T(4,128)(2,1)}), bf16[4,128,1024]{2,0,1:T(4,128)(2,1)S(1)}, u32[]{:S(2)}, u32[]{:S(2)}) async-start(bf16[4,128,1024]{2,0,1:T(4,128)(2,1)} %copy.58), calls=%async_computation | async-start | bytes 2097152 | tf_op jit(solution)/shard_map/all_to_all | solution.py:35
  40.4 30.9 %all-to-all-start.2 = ((bf16[8,64,1024]{2,0,1:T(8,128)(2,1)}), bf16[8,64,1024]{2,0,1:T(8,128)(2,1)}, u32[]{:S(2)}, u32[]{:S(2)}) async-start(bf16[8,64,1024]{2,0,1:T(8,128)(2,1)} %copy.64), calls=%async_computation.2 | async-start | bytes 2097152 | tf_op jit(solution)/shard_map/all_to_all | solution.py:50
  57.9 7.6 %copy-start.2 = (bf16[64,4,2,1024]{3,0,2,1:T(8,128)(2,1)}, bf16[64,4,2,1024]{3,0,2,1:T(8,128)(2,1)S(1)}, u32[]{:S(2)}) copy-start(bf16[64,4,2,1024]{3,0,2,1:T(8,128)(2,1)S(1)} %reshape.51) | copy-start | bytes 3145732
  71.3 10.9 %copy-start.5 = (bf16[4,128,512]{2,1,0:T(8,128)(2,1)S(1)}, bf16[4,128,512]{2,1,0:T(8,128)(2,1)}, u32[]{:S(2)}) copy-start(bf16[4,128,512]{2,1,0:T(8,128)(2,1)} %param.9) | copy-start | bytes 1572868
  80.2 2.0 copy-start.1
  85.2 33.0 %all-to-all-start.3 = ((bf16[8,64,1024]{2,0,1:T(8,128)(2,1)}), bf16[8,64,1024]{2,0,1:T(8,128)(2,1)S(1)}, u32[]{:S(2)}, u32[]{:S(2)}) async-start(bf16[8,64,1024]{2,0,1:T(8,128)(2,1)} %copy.67), calls=%async_computation.3 | async-start | bytes 2097152 | tf_op jit(solution)/shard_map/all_to_all | solution.py:68
  118.2 33.1 %all-to-all-start.1 = ((bf16[4,128,1024]{2,0,1:T(4,128)(2,1)}), bf16[4,128,1024]{2,0,1:T(4,128)(2,1)}, u32[]{:S(2)}, u32[]{:S(2)}) async-start(bf16[4,128,1024]{2,0,1:T(4,128)(2,1)} %copy.60), calls=%async_computation.1 | async-start | bytes 2097152 | tf_op jit(solution)/shard_map/all_to_all | solution.py:44
  135.2 217.8 %all-reduce.3.cloned.1.call-start = ((), (), s32[]{:S(2)}) async-start(), calls=%async_computation.4 | async-start | bytes 5242880 | tf_op jit(solution)/shard_map/psum | solution.py:74
  144.7 14.5 %copy-start.3 = (bf16[4,128,128]{2,1,0:T(8,128)(2,1)S(1)}, bf16[4,128,128]{2,1,0:T(8,128)(2,1)}, u32[]{:S(2)}) copy-start(bf16[4,128,128]{2,1,0:T(8,128)(2,1)} %param.8) | copy-start | bytes 393220
Sparse Core Ops, SparseCore 0:
  159.3 193.6 all-reduce.2
where the time goes:
time: 367 us; the launch traced here: 366 us
  waiting for transfers between devices  223 us (61%)
  starting transfers between devices  60.5 us (16%)
  matrix products  39.2 us (11%)
  local copies, waits for them, and re-layouts  29 us (8%)
  between operations  14.2 us (4%)
    psum x1, waiting for transfers between devices, local(): lax.psum((first_grad, second_grad, third_grad, fourth_grad), 'dp')  189 us
    all_to_all x1, starting transfers between devices, local(): lax.all_to_all(third_out, 'factor', split_axis=1, concat_axis=0, tiled=True)  17 us
    all_to_all x1, starting transfers between devices, local(): lax.all_to_all(first_sent, 'factor', split_axis=1, concat_axis=0, tiled=T...  17 us
    all_to_all x1, starting transfers between devices, local(): lax.all_to_all(grad_sent, 'factor', split_axis=1, concat_axis=0, tiled=True)  14.8 us
    all_to_all x1, waiting for transfers between devices, local(): lax.all_to_all(first_out, 'factor', split_axis=1, concat_axis=0, tiled=True)  14 us
    all_to_all x1, starting transfers between devices, local(): lax.all_to_all(first_out, 'factor', split_axis=1, concat_axis=0, tiled=True)  11.5 us
    dot_general x1, matrix products, local(): jnp.einsum('kbt,bhk->tbh', back_two, third_factor, preferred_element_type...  8.9 us
    all_to_all x1, waiting for transfers between devices, local(): lax.all_to_all(first_sent, 'factor', split_axis=1, concat_axis=0, tiled=T...  8.84 us
  transfers between devices with their start and end apart: 5, of which 5 were waited for; matrix products, arithmetic and copies ran while one was open for 10% of the time, Pallas kernels for 0%

commit v1 on v0

v1 whole, which is shorter than its diff:
```python
import functools
import math

import jax
import jax.numpy as jnp
from jax import lax
from jax.experimental import pallas as pl
from jax.experimental.pallas import tpu as pltpu
from jax.sharding import PartitionSpec as P

BF = jnp.bfloat16
F32 = jnp.float32
CHUNKS = 4
SIDE = 4
HALF = 8
SCALE = math.sqrt(2.0 / math.pi)
CUBE = 0.044715


def nn(a, b):
    return lax.dot_general(a, b, (((1,), (0,)), ((), ())), preferred_element_type=F32)


def nt(a, b):
    return lax.dot_general(a, b, (((1,), (1,)), ((), ())), preferred_element_type=F32)


def tn(a, b):
    return lax.dot_general(a, b, (((0,), (0,)), ((), ())), preferred_element_type=F32)


def iotas(rows, cols, flip):
    axis = 1 if flip else 0
    shape = (cols, rows) if flip else (rows, cols)
    return (
        lax.broadcasted_iota(jnp.int32, shape, axis),
        lax.broadcasted_iota(jnp.int32, shape, 1 - axis),
    )


def one_hot(keep):
    return jnp.where(keep, 1.0, 0.0).astype(BF)


def pick_first(j, flip=False):
    row, k = iotas(512, 128, flip)
    return one_hot(
        (((row >> 2) & 3) == j) & (k == (row >> 5) * 8 + ((row >> 4) & 1) * 4 + (row & 3))
    )


def pick_second(half, flip=False):
    row, m = iotas(256, 128, flip)
    return one_hot((((row >> 1) & 1) == half) & (m == (row & 1) * 64 + (row >> 2)))


def pick_third(half, flip=False):
    row, k = iotas(256, 128, flip)
    return one_hot((((row >> 3) & 1) == half) & (k == (row >> 4) * 8 + (row & 7)))


def pick_fourth(c, flip=False):
    row, m = iotas(512, 128, flip)
    return one_hot(
        (((row >> 1) & 3) == c) & (m == (row & 1) * 64 + (row >> 5) * 4 + ((row >> 3) & 3))
    )


def kernel(
    x_hbm, cot_hbm, w1_hbm, w2_hbm, w3_hbm, w4_hbm,
    res_hbm, ig_hbm, g1_ref, g2_ref, g3_ref, g4_ref,
    x, cot, w1, w2, w3, w4,
    w1r, w4r, w2r, w2t, w3r, w3t,
    send_a, recv_a, send_b, recv_b, send_c, recv_c, send_d, recv_d,
    hidden, slope, grad_pre, res, ig,
    s1, s2, s3, s4,
    y_send, y_recv, z_send, z_recv, z_own,
    y4_send, y4_recv, z4_send, z4_recv, z4_own,
    t_send, t_recv,
    load_sem, store_sem, a2a_send, a2a_recv, rs_send, rs_recv,
):
    tokens = x.shape[1]
    me = lax.axis_index("factor")
    dp = lax.axis_index("dp")
    half, low = me // HALF, me % HALF
    row, col = dp // SIDE, dp % SIDE

    barrier = pltpu.get_barrier_semaphore()

    def greet(i, _):
        pl.semaphore_signal(barrier, inc=1, device_id={"factor": (me + i) % 16}, device_id_type=pl.DeviceIdType.MESH)
        pl.semaphore_signal(barrier, inc=1, device_id={"dp": (dp + i) % 16}, device_id_type=pl.DeviceIdType.MESH)
        return 0

    lax.fori_loop(1, 16, greet, 0)

    loads = []

    def load(src, dst):
        copy = pltpu.make_async_copy(src, dst, load_sem.at[len(loads)])
        copy.start()
        loads.append(copy)
        return copy

    got_w1 = load(w1_hbm, w1)
    got_x = [load(x_hbm.at[pl.ds(c * tokens, tokens)], x.at[c]) for c in range(CHUNKS)]
    got_w4 = load(w4_hbm, w4)
    got_cot = [load(cot_hbm.at[pl.ds(c * tokens, tokens)], cot.at[c]) for c in range(CHUNKS)]
    got_w2 = load(w2_hbm, w2)
    got_w3 = load(w3_hbm, w3)

    def spread(phase, c, send, recv):
        recv[c, me] = send[c, me]

        def one(peer):
            pltpu.make_async_remote_copy(
                src_ref=send.at[c, peer], dst_ref=recv.at[c, me],
                send_sem=a2a_send.at[phase, c], recv_sem=a2a_recv.at[phase, c],
                device_id={"factor": peer}, device_id_type=pl.DeviceIdType.MESH,
            ).start()

        def far(i, _):
            one((1 - half) * HALF + (low + i) % HALF)
            return 0

        def near(i, _):
            one(half * HALF + (low + i) % HALF)
            return 0

        lax.fori_loop(0, HALF, far, 0)
        lax.fori_loop(1, HALF, near, 0)

    def wait_bytes(ref, sem):
        pltpu.make_async_copy(ref, ref, sem).wait()

    def arrived(phase, c, recv):
        wait_bytes(recv.at[c, pl.ds(0, 15)], a2a_recv.at[phase, c])

    got_w1.wait()
    for j in range(4):
        w1r[:, j * 128 : (j + 1) * 128] = nt(pick_first(j), w1[j]).astype(BF)
    for c in range(CHUNKS):
        got_x[c].wait()
        send_a[c] = nt(w1r[...], x[c]).astype(BF).reshape(16, 32, tokens)
        if c == 0:
            pl.semaphore_wait(barrier, 30)
        spread(0, c, send_a, recv_a)

    got_w4.wait()
    for c in range(4):
        w4r[:, c * 128 : (c + 1) * 128] = nn(pick_fourth(c), w4[c]).astype(BF)
    for c in range(CHUNKS):
        got_cot[c].wait()
        send_b[c] = nt(w4r[...], cot[c]).astype(BF).reshape(16, 32, tokens)
        spread(1, c, send_b, recv_b)

    got_w2.wait()
    got_w3.wait()
    for p in range(2):
        for h in range(2):
            b = 2 * p + h
            w2r[p, :, h * 512 : (h + 1) * 512] = nn(pick_second(h), w2[b]).astype(BF)
            w2t[p, h * 512 : (h + 1) * 512, :] = tn(w2[b], pick_second(h, True)).astype(BF)
            w3r[p, h * 512 : (h + 1) * 512, :] = nn(w3[b], pick_third(h, True)).astype(BF)
            w3t[p, :, h * 512 : (h + 1) * 512] = nt(pick_third(h), w3[b]).astype(BF)
    s1[...] = jnp.zeros_like(s1)
    s2[...] = jnp.zeros_like(s2)
    s3[...] = jnp.zeros_like(s3)
    s4[...] = jnp.zeros_like(s4)

    def pair_rows(ref, c, p):
        return ref[c, :, pl.ds(p * 16, 16), :].reshape(256, tokens)

    def forward(c, _):
        arrived(0, c, recv_a)
        for p in range(2):
            mixed = pair_rows(recv_a, c, p)

            def tile(o, _):
                at = pl.ds(pl.multiple_of(o * 256, 256), 256)
                v = nn(w2t[p, at, :], mixed)
                sq = v * v
                t = jnp.tanh(v * (SCALE + (SCALE * CUBE) * sq))
                cdf = 0.5 + 0.5 * t
                hidden[c, p, at, :] = (v * cdf).astype(BF)
                slope[c, p, at, :] = cdf + (0.5 * v) * (1.0 - t * t) * (SCALE + (3.0 * SCALE * CUBE) * sq)
                return 0

            lax.fori_loop(0, 4, tile, 0)
            third = nn(w3t[p], hidden[c, p]).astype(BF)
            send_c[c, :, p * 16 : (p + 1) * 16, :] = third.reshape(16, 16, tokens)
        spread(2, c, send_c, recv_c)
        return 0

    lax.fori_loop(0, CHUNKS, forward, 0)

    def backward(c, _):
        arrived(1, c, recv_b)
        for p in range(2):
            back = pair_rows(recv_b, c, p)

            def tile(o, _):
                at = pl.ds(pl.multiple_of(o * 256, 256), 256)
                grad_pre[p, at, :] = (nn(w3r[p, at, :], back) * slope[c, p, at, :]).astype(BF)
                return 0

            lax.fori_loop(0, 4, tile, 0)
            first = nn(w2r[p], grad_pre[p]).astype(BF)
            send_d[c, :, p * 16 : (p + 1) * 16, :] = first.reshape(16, 16, tokens)
        spread(3, c, send_d, recv_d)
        for p in range(2):
            back = pair_rows(recv_b, c, p)
            mixed = pair_rows(recv_a, c, p)

            def sums(o, _):
                at = pl.ds(pl.multiple_of(o * 256, 256), 256)
                s3[p, at, :] += nt(hidden[c, p, at, :], back)
                s2[p, o] += nt(mixed, grad_pre[p, at, :])
                return 0

            lax.fori_loop(0, 4, sums, 0)
        return 0

    lax.fori_loop(0, CHUNKS, backward, 0)

    def scatter(n, axis, at, members, stride, base, send, recv):
        def one(i, _):
            peer = (at + i) % members
            pltpu.make_async_remote_copy(
                src_ref=send.at[peer], dst_ref=recv.at[at],
                send_sem=rs_send.at[n], recv_sem=rs_recv.at[n],
                device_id={"dp": base + peer * stride}, device_id_type=pl.DeviceIdType.MESH,
            ).start()
            return 0

        lax.fori_loop(1, members, one, 0)

    def scatter_y(n, send, recv):
        scatter(n, "y", row, SIDE, SIDE, col, send, recv)

    def scatter_z(n, send, recv):
        scatter(n, "z", col, SIDE, 1, row * SIDE, send, recv)

    for b in range(4):
        p, h = b // 2, b % 2
        third = s3[p, h * 512 : (h + 1) * 512, :].astype(BF)
        y_send[:, 1, :, b * 128 : (b + 1) * 128] = (
            nn(third, pick_third(h)).astype(BF).reshape(4, 128, 128)
        )
    for o in range(2):
        parts = [
            nn(pick_second(b % 2, True), s2[b // 2, 2 * (b % 2) + o].astype(BF)).reshape(16, 1, 8, 256)
            for b in range(4)
        ]
        y_send[:, 0, :, o * 256 : (o + 1) * 256] = (
            jnp.concatenate(parts, axis=1).reshape(4, 128, 256).astype(BF)
        )
    scatter_y(0, y_send, y_recv)

    def last_forward(c, _):
        arrived(2, c, recv_c)
        mixed = recv_c[c].reshape(512, tokens)
        res[c] = tn(mixed, w4r[...]).astype(BF)
        at = pl.ds(pl.multiple_of(c * tokens, tokens), tokens)
        pltpu.make_async_copy(res.at[c], res_hbm.at[at], store_sem.at[0, c]).start()
        s4[...] += nn(mixed, cot[c])
        return 0

    lax.fori_loop(0, CHUNKS, last_forward, 0)

    def own_rows(parts):
        return jnp.concatenate([v.reshape(16, 1, 8, 128) for v in parts], axis=1)

    parts = [nn(pick_fourth(c, True), s4[:, c * 128 : (c + 1) * 128].astype(BF)) for c in range(4)]
    y4_send[...] = own_rows(parts).reshape(4, 128, 128).astype(BF)
    scatter_y(1, y4_send, y4_recv)

    wait_bytes(y_recv.at[pl.ds(0, SIDE - 1)], rs_recv.at[0])
    for n in range(2):
        total = y_send[row, n].astype(F32)
        for i in range(1, SIDE):
            total += y_recv[(row + i) % SIDE, n].astype(F32)
        z_send[:, n] = total.astype(BF).reshape(SIDE, 32, 512)
        z_own[:, n] = total.reshape(SIDE, 32, 512)
    scatter_z(2, z_send, z_recv)

    def last_backward(c, _):
        arrived(3, c, recv_d)
        mixed = recv_d[c].reshape(512, tokens)
        ig[c] = tn(mixed, w1r[...]).astype(BF)
        at = pl.ds(pl.multiple_of(c * tokens, tokens), tokens)
        pltpu.make_async_copy(ig.at[c], ig_hbm.at[at], store_sem.at[1, c]).start()
        s1[...] += nn(mixed, x[c])
        return 0

    lax.fori_loop(0, CHUNKS - 1, last_backward, 0)

    wait_bytes(y4_recv.at[pl.ds(0, SIDE - 1)], rs_recv.at[1])
    total = y4_send[row].astype(F32)
    for i in range(1, SIDE):
        total += y4_recv[(row + i) % SIDE].astype(F32)
    z4_send[...] = total.astype(BF).reshape(SIDE, 32, 128)
    z4_own[...] = total.reshape(SIDE, 32, 128)
    scatter_z(3, z4_send, z4_recv)

    lax.fori_loop(CHUNKS - 1, CHUNKS, last_backward, 0)

    parts = [tn(s1[:, j * 128 : (j + 1) * 128].astype(BF), pick_first(j)) for j in range(4)]
    t_send[...] = own_rows(parts).reshape(16, 32, 128).astype(BF)
    scatter(4, "dp", dp, 16, 1, 0, t_send, t_recv)

    wait_bytes(z_recv.at[pl.ds(0, SIDE - 1)], rs_recv.at[2])
    total = z_own[col]
    for i in range(1, SIDE):
        total += z_recv[(col + i) % SIDE].astype(F32)
    g2_ref[...] = total[0].reshape(4, 8, 512)
    for j in range(4):
        g3_ref[j] = total[1, :, j * 128 : (j + 1) * 128]

    wait_bytes(z4_recv.at[pl.ds(0, SIDE - 1)], rs_recv.at[3])
    total = z4_own[col]
    for i in range(1, SIDE):
        total += z4_recv[(col + i) % SIDE].astype(F32)
    g4_ref[...] = total.reshape(4, 8, 128)

    wait_bytes(t_recv.at[pl.ds(0, 15)], rs_recv.at[4])
    total = t_send[dp].astype(F32)
    for i in range(1, 16):
        total += t_recv[(dp + i) % 16].astype(F32)
    g1_ref[...] = total.reshape(4, 8, 128)

    for c in range(CHUNKS):
        at = pl.ds(c * tokens, tokens)
        pltpu.make_async_copy(res.at[c], res_hbm.at[at], store_sem.at[0, c]).wait()
        pltpu.make_async_copy(ig.at[c], ig_hbm.at[at], store_sem.at[1, c]).wait()
        for phase, send in enumerate((send_a, send_b, send_c, send_d)):
            wait_bytes(send.at[c, pl.ds(0, 15)], a2a_send.at[phase, c])
    wait_bytes(y_send.at[pl.ds(0, SIDE - 1)], rs_send.at[0])
    wait_bytes(y4_send.at[pl.ds(0, SIDE - 1)], rs_send.at[1])
    wait_bytes(z_send.at[pl.ds(0, SIDE - 1)], rs_send.at[2])
    wait_bytes(z4_send.at[pl.ds(0, SIDE - 1)], rs_send.at[3])
    wait_bytes(t_send.at[pl.ds(0, 15)], rs_send.at[4])


def local(inputs, cotangent, first_factor, second_factor, third_factor, fourth_factor):
    count, width = inputs.shape
    tokens = count // CHUNKS
    any_spec = pl.BlockSpec(memory_space=pl.ANY)
    vmem = pl.BlockSpec(memory_space=pltpu.VMEM)
    packet = pltpu.VMEM((CHUNKS, 16, 32, tokens), BF)
    block = pltpu.VMEM((CHUNKS, tokens, width), BF)
    return pl.pallas_call(
        kernel,
        out_shape=(
            jax.ShapeDtypeStruct((count, width), BF),
            jax.ShapeDtypeStruct((count, width), BF),
            jax.ShapeDtypeStruct((4, 8, 128), F32),
            jax.ShapeDtypeStruct((4, 8, 512), F32),
            jax.ShapeDtypeStruct((4, 32, 128), F32),
            jax.ShapeDtypeStruct((4, 8, 128), F32),
        ),
        in_specs=[any_spec] * 6,
        out_specs=(any_spec, any_spec, vmem, vmem, vmem, vmem),
        scratch_shapes=[
            block, block,
            pltpu.VMEM((4, 128, 128), BF), pltpu.VMEM((4, 128, 512), BF),
            pltpu.VMEM((4, 512, 128), BF), pltpu.VMEM((4, 128, 128), BF),
            pltpu.VMEM((512, 512), BF), pltpu.VMEM((512, 512), BF),
            pltpu.VMEM((2, 256, 1024), BF), pltpu.VMEM((2, 1024, 256), BF),
            pltpu.VMEM((2, 1024, 256), BF), pltpu.VMEM((2, 256, 1024), BF),
            packet, packet, packet, packet, packet, packet, packet, packet,
            pltpu.VMEM((CHUNKS, 2, 1024, tokens), BF), pltpu.VMEM((CHUNKS, 2, 1024, tokens), F32),
            pltpu.VMEM((2, 1024, tokens), BF), block, block,
            pltpu.VMEM((512, 512), F32), pltpu.VMEM((2, 4, 256, 256), F32),
            pltpu.VMEM((2, 1024, 256), F32), pltpu.VMEM((512, 512), F32),
            pltpu.VMEM((SIDE, 2, 128, 512), BF), pltpu.VMEM((SIDE, 2, 128, 512), BF),
            pltpu.VMEM((SIDE, 2, 32, 512), BF), pltpu.VMEM((SIDE, 2, 32, 512), BF),
            pltpu.VMEM((SIDE, 2, 32, 512), F32),
            pltpu.VMEM((SIDE, 128, 128), BF), pltpu.VMEM((SIDE, 128, 128), BF),
            pltpu.VMEM((SIDE, 32, 128), BF), pltpu.VMEM((SIDE, 32, 128), BF),
            pltpu.VMEM((SIDE, 32, 128), F32),
            pltpu.VMEM((16, 32, 128), BF), pltpu.VMEM((16, 32, 128), BF),
            pltpu.SemaphoreType.DMA((2 * CHUNKS + 4,)), pltpu.SemaphoreType.DMA((2, CHUNKS)),
            pltpu.SemaphoreType.DMA((4, CHUNKS)), pltpu.SemaphoreType.DMA((4, CHUNKS)),
            pltpu.SemaphoreType.DMA((5,)), pltpu.SemaphoreType.DMA((5,)),
        ],
        compiler_params=pltpu.CompilerParams(
            collective_id=0, has_side_effects=True, vmem_limit_bytes=56 * 2**20
        ),
        cost_estimate=pl.CostEstimate(flops=8 * 10**9, bytes_accessed=6 * 10**6, transcendentals=2 * 10**6),
    )(inputs, cotangent, first_factor, second_factor, third_factor, fourth_factor)


def solution(mesh):
    in_specs = (
        P("dp", "factor"),
        P("dp", "factor"),
        P("factor", None, None),
        P("factor", None, None),
        P("factor", None, None),
        P("factor", None, None),
    )
    out_specs = (
        P("dp", "factor"),
        P("dp", "factor"),
        P("factor", "dp", None),
        P("factor", "dp", None),
        P("factor", "dp", None),
        P("factor", "dp", None),
    )
    return jax.shard_map(local, mesh=mesh, in_specs=in_specs, out_specs=out_specs, check_vma=False)
```

time: 367 us -> 122 us (0.33)
  waiting for transfers between devices: 223 us -> 0 us
  Pallas kernels: 0 us -> 114 us
  starting transfers between devices: 60.5 us -> 0 us
  matrix products: 39.2 us -> 0 us
  local copies, waits for them, and re-layouts: 29 us -> 6.12 us
  between operations: 14.2 us -> 0.66 us
    psum x1 -> x0, waiting for transfers between devices: 189 us -> none  [local(): lax.psum((first_grad, second_grad, third_grad, fourth_grad), 'dp')]
    pallas_call x0 -> x1, Pallas kernels: none -> 114 us  [local(): pl.pallas_call(kernel, out_shape=(jax.ShapeDtypeStruct((count, width), BF...]
    all_to_all x4 -> x0, starting transfers between devices: 60.3 us -> none  [the longest x1 17 us: local(): lax.all_to_all(third_out, 'factor', split_axis=1, concat_axis=0, tiled=True)]
    dot_general x12 -> x0, matrix products: 39.2 us -> none  [the longest x1 8.9 us: local(): jnp.einsum('kbt,bhk->tbh', back_two, third_factor, preferred_element_type...]
    all_to_all x4 -> x0, waiting for transfers between devices: 34.1 us -> none  [the longest x1 14 us: local(): lax.all_to_all(first_out, 'factor', split_axis=1, concat_axis=0, tiled=True)]
    reshape x5 -> x0, local copies, waits for them, and re-layouts: 7.91 us -> none  [the longest x1 2.13 us: local(): third_view = third_mixed.reshape(blocks, local_blocks, stride, count)]
    dynamic_slice x4 -> x0, local copies, waits for them, and re-layouts: 5.34 us -> none  [own_rows(): return lax.dynamic_slice_in_dim(values, position * rows, rows, 1)]
    all_to_all x3 -> x0, local copies, waits for them, and re-layouts: 4.73 us -> none  [the longest x2 3.32 us: local(): lax.all_to_all(third_out, 'factor', split_axis=1, concat_axis=0, tiled=True)]
  transfers between devices with their start and end apart: 5 -> 0, of which waited for: 5 -> 0; matrix products, arithmetic and copies ran while one was open for 10% -> 0% of each run, Pallas kernels for 0% -> 0%
where the time goes in v1:
time: 122 us; the launch traced here: 121 us
  Pallas kernels  114 us (93%)
  local copies, waits for them, and re-layouts  6.12 us (5%)
    pallas_call x1, Pallas kernels, local(): pl.pallas_call(kernel, out_shape=(jax.ShapeDtypeStruct((count, width), BF...  114 us
    unnamed x16, local copies, waits for them, and re-layouts  6.12 us

profile of v1, /device:TPU:2, one launch (start us, length us, event | category | flops | bytes accessed | tf_op | source)
XLA Modules:
  0.0 120.7 jit_solution(3938849851482045278)
XLA Ops:
  0.6 113.9 %shard_map.109 = (bf16[1024,512]{1,0:T(8,128)(2,1)}, bf16[1024,512]{1,0:T(8,128)(2,1)}, f32[4,8,128]{2,1,0:T(8,128)}, f32[4,8,512]{2,1,0:T(8,128)}, f32[4,32,128]{2,1,0:T(8,128)}, /*index=5*/f32[4,8,128]{2,1,0:T(8,128)}) custom-call(bf16[1024,512]{1,0:T(8,128)(2,1)} %x_hbm.1, bf16[1024,512]{1,0:T(8,128)(2,1)} %cot_hbm.1, bf16[4,128,128]{2,1,0:T(8,128)(2,1)} %w1_hbm.1, ...), custom_call_target="tpu_custom_call" | custom-call | flops 8000000000 | bytes 6000000 | tf_op jit(solution)/shard_map/pallas_call | solution.py:352
  114.5 0.0 copy-start
  114.6 2.4 %copy.18 = bf16[1024,512]{1,0:T(8,128)(2,1)} copy(bf16[1024,512]{1,0:T(8,128)(2,1)} %get-tuple-element.12) | data formatting | bytes 2097152
  116.9 0.0 copy-done
  116.9 0.0 copy-start.4
  116.9 0.0 copy-start.2
  116.9 1.0 copy.19
  117.9 0.0 copy-done.4
  117.9 0.6 copy.20
  118.5 0.0 copy-done.2
  118.5 0.0 copy-start.1
  118.5 0.6 copy.21
  119.1 0.2 copy-done.1
  119.4 0.0 copy-start.3
  119.4 0.6 copy.22
  120.0 0.1 copy-done.3
  120.1 0.6 copy.23
Async XLA Ops:
  114.5 2.4 %copy-start = (bf16[1024,512]{1,0:T(8,128)(2,1)S(1)}, bf16[1024,512]{1,0:T(8,128)(2,1)}, u32[]{:S(2)}) copy-start(bf16[1024,512]{1,0:T(8,128)(2,1)} %get-tuple-element.13) | copy-start | bytes 3145732
  116.9 1.0 copy-start.4
  116.9 1.6 %copy-start.2 = (f32[4,8,512]{2,1,0:T(8,128)S(1)}, f32[4,8,512]{2,1,0:T(8,128)}, u32[]{:S(2)}) copy-start(f32[4,8,512]{2,1,0:T(8,128)} %get-tuple-element.15) | copy-start | bytes 196612
  118.5 0.9 copy-start.1
  119.4 0.7 copy-start.3

commit v2 on v1

--- a/solution.py
+++ b/solution.py
@@ -76,7 +76,7 @@
     s1, s2, s3, s4,
     y_send, y_recv, z_send, z_recv, z_own,
     y4_send, y4_recv, z4_send, z4_recv, z4_own,
-    t_send, t_recv,
+    y1_send, y1_recv, z1_send, z1_recv, z1_own,
     load_sem, store_sem, a2a_send, a2a_recv, rs_send, rs_recv,
 ):
     tokens = x.shape[1]
@@ -88,8 +88,8 @@
     barrier = pltpu.get_barrier_semaphore()
 
     def greet(i, _):
-        pl.semaphore_signal(barrier, inc=1, device_id={"factor": (me + i) % 16}, device_id_type=pl.DeviceIdType.MESH)
-        pl.semaphore_signal(barrier, inc=1, device_id={"dp": (dp + i) % 16}, device_id_type=pl.DeviceIdType.MESH)
+        for peer in ({"factor": (me + i) % 16}, {"dp": (dp + i) % 16}):
+            pl.semaphore_signal(barrier, inc=1, device_id=peer, device_id_type=pl.DeviceIdType.MESH)
         return 0
 
     lax.fori_loop(1, 16, greet, 0)
@@ -223,7 +223,7 @@
 
     lax.fori_loop(0, CHUNKS, backward, 0)
 
-    def scatter(n, axis, at, members, stride, base, send, recv):
+    def scatter(n, at, members, stride, base, send, recv):
         def one(i, _):
             peer = (at + i) % members
             pltpu.make_async_remote_copy(
@@ -236,10 +236,10 @@
         lax.fori_loop(1, members, one, 0)
 
     def scatter_y(n, send, recv):
-        scatter(n, "y", row, SIDE, SIDE, col, send, recv)
+        scatter(n, row, SIDE, SIDE, col, send, recv)
 
     def scatter_z(n, send, recv):
-        scatter(n, "z", col, SIDE, 1, row * SIDE, send, recv)
+        scatter(n, col, SIDE, 1, row * SIDE, send, recv)
 
     for b in range(4):
         p, h = b // 2, b % 2
@@ -280,54 +280,61 @@
         total = y_send[row, n].astype(F32)
         for i in range(1, SIDE):
             total += y_recv[(row + i) % SIDE, n].astype(F32)
-        z_send[:, n] = total.astype(BF).reshape(SIDE, 32, 512)
-        z_own[:, n] = total.reshape(SIDE, 32, 512)
-    scatter_z(2, z_send, z_recv)
+        z_send[n] = total.astype(BF).reshape(SIDE, 32, 512)
+        z_own[n] = total.reshape(SIDE, 32, 512)
+
+    def input_rows(c):
+        ig[c] = tn(recv_d[c].reshape(512, tokens), w1r[...]).astype(BF)
+        at = pl.ds(pl.multiple_of(c * tokens, tokens), tokens)
+        pltpu.make_async_copy(ig.at[c], ig_hbm.at[at], store_sem.at[1, c]).start()
 
     def last_backward(c, _):
         arrived(3, c, recv_d)
-        mixed = recv_d[c].reshape(512, tokens)
-        ig[c] = tn(mixed, w1r[...]).astype(BF)
-        at = pl.ds(pl.multiple_of(c * tokens, tokens), tokens)
-        pltpu.make_async_copy(ig.at[c], ig_hbm.at[at], store_sem.at[1, c]).start()
-        s1[...] += nn(mixed, x[c])
+        s1[...] += nn(recv_d[c].reshape(512, tokens), x[c])
+        input_rows(c)
         return 0
 
     lax.fori_loop(0, CHUNKS - 1, last_backward, 0)
 
-    wait_bytes(y4_recv.at[pl.ds(0, SIDE - 1)], rs_recv.at[1])
-    total = y4_send[row].astype(F32)
-    for i in range(1, SIDE):
-        total += y4_recv[(row + i) % SIDE].astype(F32)
-    z4_send[...] = total.astype(BF).reshape(SIDE, 32, 128)
-    z4_own[...] = total.reshape(SIDE, 32, 128)
+    def fold(n, y_out, y_in, z_out, own):
+        wait_bytes(y_in.at[pl.ds(0, SIDE - 1)], rs_recv.at[n])
+        total = y_out[row].astype(F32)
+        for i in range(1, SIDE):
+            total += y_in[(row + i) % SIDE].astype(F32)
+        z_out[...] = total.astype(BF).reshape(SIDE, 32, 128)
+        own[...] = total.reshape(SIDE, 32, 128)
+
+    fold(1, y4_send, y4_recv, z4_send, z4_own)
+
+    arrived(3, CHUNKS - 1, recv_d)
+    scatter_z(2, z_send.at[0], z_recv.at[0])
+    scatter_z(5, z_send.at[1], z_recv.at[1])
     scatter_z(3, z4_send, z4_recv)
-
-    lax.fori_loop(CHUNKS - 1, CHUNKS, last_backward, 0)
-
+    s1[...] += nn(recv_d[CHUNKS - 1].reshape(512, tokens), x[CHUNKS - 1])
     parts = [tn(s1[:, j * 128 : (j + 1) * 128].astype(BF), pick_first(j)) for j in range(4)]
-    t_send[...] = own_rows(parts).reshape(16, 32, 128).astype(BF)
-    scatter(4, "dp", dp, 16, 1, 0, t_send, t_recv)
-
-    wait_bytes(z_recv.at[pl.ds(0, SIDE - 1)], rs_recv.at[2])
-    total = z_own[col]
-    for i in range(1, SIDE):
-        total += z_recv[(col + i) % SIDE].astype(F32)
-    g2_ref[...] = total[0].reshape(4, 8, 512)
-    for j in range(4):
-        g3_ref[j] = total[1, :, j * 128 : (j + 1) * 128]
-
-    wait_bytes(z4_recv.at[pl.ds(0, SIDE - 1)], rs_recv.at[3])
-    total = z4_own[col]
-    for i in range(1, SIDE):
-        total += z4_recv[(col + i) % SIDE].astype(F32)
-    g4_ref[...] = total.reshape(4, 8, 128)
-
-    wait_bytes(t_recv.at[pl.ds(0, 15)], rs_recv.at[4])
-    total = t_send[dp].astype(F32)
-    for i in range(1, 16):
-        total += t_recv[(dp + i) % 16].astype(F32)
-    g1_ref[...] = total.reshape(4, 8, 128)
+    y1_send[...] = own_rows(parts).reshape(4, 128, 128).astype(BF)
+    scatter_y(4, y1_send, y1_recv)
+    input_rows(CHUNKS - 1)
+    fold(4, y1_send, y1_recv, z1_send, z1_own)
+    scatter_z(6, z1_send, z1_recv)
+
+    for n in range(2):
+        wait_bytes(z_recv.at[n, pl.ds(0, SIDE - 1)], rs_recv.at[(2, 5)[n]])
+        total = z_own[n, col]
+        for i in range(1, SIDE):
+            total += z_recv[n, (col + i) % SIDE].astype(F32)
+        if n == 0:
+            g2_ref[...] = total.reshape(4, 8, 512)
+        else:
+            for j in range(4):
+                g3_ref[j] = total[:, j * 128 : (j + 1) * 128]
+
+    for n, own, recv, out in ((3, z4_own, z4_recv, g4_ref), (6, z1_own, z1_recv, g1_ref)):
+        wait_bytes(recv.at[pl.ds(0, SIDE - 1)], rs_recv.at[n])
+        total = own[col]
+        for i in range(1, SIDE):
+            total += recv[(col + i) % SIDE].astype(F32)
+        out[...] = total.reshape(4, 8, 128)
 
     for c in range(CHUNKS):
         at = pl.ds(c * tokens, tokens)
@@ -337,9 +344,33 @@
             wait_bytes(send.at[c, pl.ds(0, 15)], a2a_send.at[phase, c])
     wait_bytes(y_send.at[pl.ds(0, SIDE - 1)], rs_send.at[0])
     wait_bytes(y4_send.at[pl.ds(0, SIDE - 1)], rs_send.at[1])
-    wait_bytes(z_send.at[pl.ds(0, SIDE - 1)], rs_send.at[2])
+    wait_bytes(z_send.at[0, pl.ds(0, SIDE - 1)], rs_send.at[2])
+    wait_bytes(z_send.at[1, pl.ds(0, SIDE - 1)], rs_send.at[5])
     wait_bytes(z4_send.at[pl.ds(0, SIDE - 1)], rs_send.at[3])
-    wait_bytes(t_send.at[pl.ds(0, 15)], rs_send.at[4])
+    wait_bytes(y1_send.at[pl.ds(0, SIDE - 1)], rs_send.at[4])
+    wait_bytes(z1_send.at[pl.ds(0, SIDE - 1)], rs_send.at[6])
+
+
+def publish(*refs):
+    sources, targets, held, sem = refs[:6], refs[6:12], refs[12:18], refs[18]
+    copies = []
+    for n, (source, target, slot) in enumerate(zip(sources, targets, held)):
+        parts = CHUNKS if n < 2 else 1
+        rows = source.shape[0] // parts
+        for i in range(parts):
+            at = pl.ds(i * rows, rows)
+            k = len(copies)
+            copies.append((
+                pltpu.make_async_copy(source.at[at], slot.at[at], sem.at[0, k]),
+                pltpu.make_async_copy(slot.at[at], target.at[at], sem.at[1, k]),
+            ))
+    for come, _ in copies:
+        come.start()
+    for come, go in copies:
+        come.wait()
+        go.start()
+    for _, go in copies:
+        go.wait()
 
 
 def local(inputs, cotangent, first_factor, second_factor, third_factor, fourth_factor):
@@ -349,16 +380,17 @@
     vmem = pl.BlockSpec(memory_space=pltpu.VMEM)
     packet = pltpu.VMEM((CHUNKS, 16, 32, tokens), BF)
     block = pltpu.VMEM((CHUNKS, tokens, width), BF)
-    return pl.pallas_call(
+    outs = (
+        jax.ShapeDtypeStruct((count, width), BF),
+        jax.ShapeDtypeStruct((count, width), BF),
+        jax.ShapeDtypeStruct((4, 8, 128), F32),
+        jax.ShapeDtypeStruct((4, 8, 512), F32),
+        jax.ShapeDtypeStruct((4, 32, 128), F32),
+        jax.ShapeDtypeStruct((4, 8, 128), F32),
+    )
+    made = pl.pallas_call(
         kernel,
-        out_shape=(
-            jax.ShapeDtypeStruct((count, width), BF),
-            jax.ShapeDtypeStruct((count, width), BF),
-            jax.ShapeDtypeStruct((4, 8, 128), F32),
-            jax.ShapeDtypeStruct((4, 8, 512), F32),
-            jax.ShapeDtypeStruct((4, 32, 128), F32),
-            jax.ShapeDtypeStruct((4, 8, 128), F32),
-        ),
+        out_shape=outs,
         in_specs=[any_spec] * 6,
         out_specs=(any_spec, any_spec, vmem, vmem, vmem, vmem),
         scratch_shapes=[
@@ -374,21 +406,32 @@
             pltpu.VMEM((512, 512), F32), pltpu.VMEM((2, 4, 256, 256), F32),
             pltpu.VMEM((2, 1024, 256), F32), pltpu.VMEM((512, 512), F32),
             pltpu.VMEM((SIDE, 2, 128, 512), BF), pltpu.VMEM((SIDE, 2, 128, 512), BF),
-            pltpu.VMEM((SIDE, 2, 32, 512), BF), pltpu.VMEM((SIDE, 2, 32, 512), BF),
-            pltpu.VMEM((SIDE, 2, 32, 512), F32),
+            pltpu.VMEM((2, SIDE, 32, 512), BF), pltpu.VMEM((2, SIDE, 32, 512), BF),
+            pltpu.VMEM((2, SIDE, 32, 512), F32),
             pltpu.VMEM((SIDE, 128, 128), BF), pltpu.VMEM((SIDE, 128, 128), BF),
             pltpu.VMEM((SIDE, 32, 128), BF), pltpu.VMEM((SIDE, 32, 128), BF),
             pltpu.VMEM((SIDE, 32, 128), F32),
-            pltpu.VMEM((16, 32, 128), BF), pltpu.VMEM((16, 32, 128), BF),
+            pltpu.VMEM((SIDE, 128, 128), BF), pltpu.VMEM((SIDE, 128, 128), BF),
+            pltpu.VMEM((SIDE, 32, 128), BF), pltpu.VMEM((SIDE, 32, 128), BF),
+            pltpu.VMEM((SIDE, 32, 128), F32),
             pltpu.SemaphoreType.DMA((2 * CHUNKS + 4,)), pltpu.SemaphoreType.DMA((2, CHUNKS)),
             pltpu.SemaphoreType.DMA((4, CHUNKS)), pltpu.SemaphoreType.DMA((4, CHUNKS)),
-            pltpu.SemaphoreType.DMA((5,)), pltpu.SemaphoreType.DMA((5,)),
+            pltpu.SemaphoreType.DMA((7,)), pltpu.SemaphoreType.DMA((7,)),
         ],
         compiler_params=pltpu.CompilerParams(
             collective_id=0, has_side_effects=True, vmem_limit_bytes=56 * 2**20
         ),
         cost_estimate=pl.CostEstimate(flops=8 * 10**9, bytes_accessed=6 * 10**6, transcendentals=2 * 10**6),
     )(inputs, cotangent, first_factor, second_factor, third_factor, fourth_factor)
+    return pl.pallas_call(
+        publish,
+        out_shape=outs,
+        in_specs=[any_spec] * 6,
+        out_specs=(any_spec,) * 6,
+        scratch_shapes=[pltpu.VMEM(out.shape, out.dtype) for out in outs]
+        + [pltpu.SemaphoreType.DMA((2, 2 * CHUNKS + 4))],
+        cost_estimate=pl.CostEstimate(flops=0, bytes_accessed=5 * 10**6, transcendentals=0),
+    )(*made)
 
 
 def solution(mesh):

time: 122 us -> 118 us (0.967)
  local copies, waits for them, and re-layouts: 6.12 us -> 0 us
  Pallas kernels: 114 us -> 116 us
    unnamed x16 -> x0, local copies, waits for them, and re-layouts: 6.12 us -> none
    pallas_call x1 -> x2, Pallas kernels: 114 us -> 116 us  [the longest x1 113 us: local(): pl.pallas_call(kernel, out_shape=outs, in_specs=[any_spec] * 6, out_specs...]
where the time goes in v2:
time: 118 us; the launch traced here: 117 us
  Pallas kernels  116 us (98%)
    pallas_call x1, Pallas kernels, local(): pl.pallas_call(kernel, out_shape=outs, in_specs=[any_spec] * 6, out_specs...  113 us
    pallas_call x1, Pallas kernels, local(): pl.pallas_call(publish, out_shape=outs, in_specs=[any_spec] * 6, out_spec...  2.51 us

profile of v2, /device:TPU:2, one launch (start us, length us, event | category | flops | bytes accessed | tf_op | source)
XLA Modules:
  0.0 116.6 jit_solution(3882835331077174359)
XLA Ops:
  0.6 113.5 %shard_map.109 = (bf16[1024,512]{1,0:T(8,128)(2,1)}, bf16[1024,512]{1,0:T(8,128)(2,1)}, f32[4,8,128]{2,1,0:T(8,128)}, f32[4,8,512]{2,1,0:T(8,128)}, f32[4,32,128]{2,1,0:T(8,128)}, /*index=5*/f32[4,8,128]{2,1,0:T(8,128)}) custom-call(bf16[1024,512]{1,0:T(8,128)(2,1)} %x_hbm.1, bf16[1024,512]{1,0:T(8,128)(2,1)} %cot_hbm.1, bf16[4,128,128]{2,1,0:T(8,128)(2,1)} %w1_hbm.1, ...), custom_call_target="tpu_custom_call" | custom-call | flops 8000000000 | bytes 6000000 | tf_op jit(solution)/shard_map/pallas_call | solution.py:391
  114.1 2.5 %shard_map.110 = (bf16[1024,512]{1,0:T(8,128)(2,1)}, bf16[1024,512]{1,0:T(8,128)(2,1)}, f32[4,8,128]{2,1,0:T(8,128)}, f32[4,8,512]{2,1,0:T(8,128)}, f32[4,32,128]{2,1,0:T(8,128)}, /*index=5*/f32[4,8,128]{2,1,0:T(8,128)}) custom-call(bf16[1024,512]{1,0:T(8,128)(2,1)} %get-tuple-element.12.refs_0_, bf16[1024,512]{1,0:T(8,128)(2,1)} %get-tuple-element.13.refs_1_, ...), custom_call_target="tpu_custom_call" | custom-call | bytes 5000000 | tf_op jit(solution)/shard_map/pallas_call | solution.py:426

commit v3 on v2

--- a/solution.py
+++ b/solution.py
@@ -10,7 +10,7 @@
 
 BF = jnp.bfloat16
 F32 = jnp.float32
-CHUNKS = 4
+CHUNKS = 2
 SIDE = 4
 HALF = 8
 SCALE = math.sqrt(2.0 / math.pi)
@@ -87,13 +87,6 @@
 
     barrier = pltpu.get_barrier_semaphore()
 
-    def greet(i, _):
-        for peer in ({"factor": (me + i) % 16}, {"dp": (dp + i) % 16}):
-            pl.semaphore_signal(barrier, inc=1, device_id=peer, device_id_type=pl.DeviceIdType.MESH)
-        return 0
-
-    lax.fori_loop(1, 16, greet, 0)
-
     loads = []
 
     def load(src, dst):
@@ -102,12 +95,23 @@
         loads.append(copy)
         return copy
 
+    def load_rows(src, dst, c):
+        return load(src.at[pl.ds(c * tokens, tokens)], dst.at[c])
+
     got_w1 = load(w1_hbm, w1)
-    got_x = [load(x_hbm.at[pl.ds(c * tokens, tokens)], x.at[c]) for c in range(CHUNKS)]
-    got_w4 = load(w4_hbm, w4)
-    got_cot = [load(cot_hbm.at[pl.ds(c * tokens, tokens)], cot.at[c]) for c in range(CHUNKS)]
-    got_w2 = load(w2_hbm, w2)
-    got_w3 = load(w3_hbm, w3)
+    got_x = [load_rows(x_hbm, x, 0)]
+
+    def greet(i, _):
+        pl.semaphore_signal(barrier, inc=1, device_id={"factor": (me + i) % 16}, device_id_type=pl.DeviceIdType.MESH)
+        return 0
+
+    def greet_dp(i, _):
+        for group in ((row + i) % SIDE * SIDE + col, row * SIDE + (col + i) % SIDE):
+            pl.semaphore_signal(barrier, inc=1, device_id={"dp": group}, device_id_type=pl.DeviceIdType.MESH)
+        return 0
+
+    lax.fori_loop(1, 16, greet, 0)
+    lax.fori_loop(1, SIDE, greet_dp, 0)
 
     def spread(phase, c, send, recv):
         recv[c, me] = send[c, me]
@@ -141,9 +145,15 @@
         w1r[:, j * 128 : (j + 1) * 128] = nt(pick_first(j), w1[j]).astype(BF)
     for c in range(CHUNKS):
         got_x[c].wait()
+        if c == 0:
+            got_x += [load_rows(x_hbm, x, n) for n in range(1, CHUNKS)]
+            got_w4 = load(w4_hbm, w4)
+            got_cot = [load_rows(cot_hbm, cot, n) for n in range(CHUNKS)]
+            got_w2 = load(w2_hbm, w2)
+            got_w3 = load(w3_hbm, w3)
         send_a[c] = nt(w1r[...], x[c]).astype(BF).reshape(16, 32, tokens)
         if c == 0:
-            pl.semaphore_wait(barrier, 30)
+            pl.semaphore_wait(barrier, 15 + 2 * (SIDE - 1))
         spread(0, c, send_a, recv_a)
 
     got_w4.wait()

time: 118 us -> 117 us (level)
  no operation moved by 1% of the time
where the time goes in v3:
time: 117 us; the launch traced here: 116 us
  Pallas kernels  115 us (98%)
    pallas_call x1, Pallas kernels, local(): pl.pallas_call(kernel, out_shape=outs, in_specs=[any_spec] * 6, out_specs...  113 us
    pallas_call x1, Pallas kernels, local(): pl.pallas_call(publish, out_shape=outs, in_specs=[any_spec] * 6, out_spec...  2.53 us

profile of v3, /device:TPU:2, one launch (start us, length us, event | category | flops | bytes accessed | tf_op | source)
XLA Modules:
  0.0 115.7 jit_solution(12796577609229858244)
XLA Ops:
  0.6 112.5 %shard_map.109 = (bf16[1024,512]{1,0:T(8,128)(2,1)}, bf16[1024,512]{1,0:T(8,128)(2,1)}, f32[4,8,128]{2,1,0:T(8,128)}, f32[4,8,512]{2,1,0:T(8,128)}, f32[4,32,128]{2,1,0:T(8,128)}, /*index=5*/f32[4,8,128]{2,1,0:T(8,128)}) custom-call(bf16[1024,512]{1,0:T(8,128)(2,1)} %x_hbm.1, bf16[1024,512]{1,0:T(8,128)(2,1)} %cot_hbm.1, bf16[4,128,128]{2,1,0:T(8,128)(2,1)} %w1_hbm.1, ...), custom_call_target="tpu_custom_call" | custom-call | flops 8000000000 | bytes 6000000 | tf_op jit(solution)/shard_map/pallas_call | solution.py:401
  113.2 2.5 %shard_map.110 = (bf16[1024,512]{1,0:T(8,128)(2,1)}, bf16[1024,512]{1,0:T(8,128)(2,1)}, f32[4,8,128]{2,1,0:T(8,128)}, f32[4,8,512]{2,1,0:T(8,128)}, f32[4,32,128]{2,1,0:T(8,128)}, /*index=5*/f32[4,8,128]{2,1,0:T(8,128)}) custom-call(bf16[1024,512]{1,0:T(8,128)(2,1)} %get-tuple-element.12.refs_0_, bf16[1024,512]{1,0:T(8,128)(2,1)} %get-tuple-element.13.refs_1_, ...), custom_call_target="tpu_custom_call" | custom-call | bytes 5000000 | tf_op jit(solution)/shard_map/pallas_call | solution.py:436

commit v4 on v3

--- a/solution.py
+++ b/solution.py
@@ -10,7 +10,8 @@
 
 BF = jnp.bfloat16
 F32 = jnp.float32
-CHUNKS = 2
+CHUNKS = 1
+PIECES = 4
 SIDE = 4
 HALF = 8
 SCALE = math.sqrt(2.0 / math.pi)
@@ -80,6 +81,7 @@
     load_sem, store_sem, a2a_send, a2a_recv, rs_send, rs_recv,
 ):
     tokens = x.shape[1]
+    piece = tokens // PIECES
     me = lax.axis_index("factor")
     dp = lax.axis_index("dp")
     half, low = me // HALF, me % HALF
@@ -99,7 +101,10 @@
         return load(src.at[pl.ds(c * tokens, tokens)], dst.at[c])
 
     got_w1 = load(w1_hbm, w1)
-    got_x = [load_rows(x_hbm, x, 0)]
+    got_first = [
+        load(x_hbm.at[pl.ds(n * piece, piece)], x.at[0, pl.ds(n * piece, piece)]) for n in range(PIECES)
+    ]
+    got_x = []
 
     def greet(i, _):
         pl.semaphore_signal(barrier, inc=1, device_id={"factor": (me + i) % 16}, device_id_type=pl.DeviceIdType.MESH)
@@ -113,26 +118,32 @@
     lax.fori_loop(1, 16, greet, 0)
     lax.fori_loop(1, SIDE, greet_dp, 0)
 
+    def send_one(phase, c, send, recv, peer):
+        pltpu.make_async_remote_copy(
+            src_ref=send.at[c, peer], dst_ref=recv.at[c, me],
+            send_sem=a2a_send.at[phase, c], recv_sem=a2a_recv.at[phase, c],
+            device_id={"factor": peer}, device_id_type=pl.DeviceIdType.MESH,
+        ).start()
+
+    def spread_far(phase, c, send, recv):
+        def far(i, _):
+            send_one(phase, c, send, recv, (1 - half) * HALF + (low + i) % HALF)
+            return 0
+
+        lax.fori_loop(0, HALF, far, 0)
+
+    def spread_near(phase, c, send, recv):
+        recv[c, me] = send[c, me]
+
+        def near(i, _):
+            send_one(phase, c, send, recv, half * HALF + (low + i) % HALF)
+            return 0
+
+        lax.fori_loop(1, HALF, near, 0)
+
     def spread(phase, c, send, recv):
-        recv[c, me] = send[c, me]
-
-        def one(peer):
-            pltpu.make_async_remote_copy(
-                src_ref=send.at[c, peer], dst_ref=recv.at[c, me],
-                send_sem=a2a_send.at[phase, c], recv_sem=a2a_recv.at[phase, c],
-                device_id={"factor": peer}, device_id_type=pl.DeviceIdType.MESH,
-            ).start()
-
-        def far(i, _):
-            one((1 - half) * HALF + (low + i) % HALF)
-            return 0
-
-        def near(i, _):
-            one(half * HALF + (low + i) % HALF)
-            return 0
-
-        lax.fori_loop(0, HALF, far, 0)
-        lax.fori_loop(1, HALF, near, 0)
+        spread_far(phase, c, send, recv)
+        spread_near(phase, c, send, recv)
 
     def wait_bytes(ref, sem):
         pltpu.make_async_copy(ref, ref, sem).wait()
@@ -143,17 +154,28 @@
     got_w1.wait()
     for j in range(4):
         w1r[:, j * 128 : (j + 1) * 128] = nt(pick_first(j), w1[j]).astype(BF)
-    for c in range(CHUNKS):
-        got_x[c].wait()
-        if c == 0:
-            got_x += [load_rows(x_hbm, x, n) for n in range(1, CHUNKS)]
-            got_w4 = load(w4_hbm, w4)
-            got_cot = [load_rows(cot_hbm, cot, n) for n in range(CHUNKS)]
-            got_w2 = load(w2_hbm, w2)
-            got_w3 = load(w3_hbm, w3)
+
+    def rows_of(side):
+        return w1r[pl.ds(pl.multiple_of(side * 256, 256), 256), :]
+
+    for n, got in enumerate(got_first):
+        got.wait()
+        at = slice(n * piece, (n + 1) * piece)
+        send_a[0, pl.ds((1 - half) * HALF, HALF), :, at] = (
+            nt(rows_of(1 - half), x[0, at]).astype(BF).reshape(HALF, 32, piece)
+        )
+    got_x += [load_rows(x_hbm, x, n) for n in range(1, CHUNKS)]
+    got_w4 = load(w4_hbm, w4)
+    got_cot = [load_rows(cot_hbm, cot, n) for n in range(CHUNKS)]
+    got_w2 = load(w2_hbm, w2)
+    got_w3 = load(w3_hbm, w3)
+    pl.semaphore_wait(barrier, 15 + 2 * (SIDE - 1))
+    spread_far(0, 0, send_a, recv_a)
+    send_a[0, pl.ds(half * HALF, HALF)] = nt(rows_of(half), x[0]).astype(BF).reshape(HALF, 32, tokens)
+    spread_near(0, 0, send_a, recv_a)
+    for c in range(1, CHUNKS):
+        got_x[c - 1].wait()
         send_a[c] = nt(w1r[...], x[c]).astype(BF).reshape(16, 32, tokens)
-        if c == 0:
-            pl.semaphore_wait(barrier, 15 + 2 * (SIDE - 1))
         spread(0, c, send_a, recv_a)
 
     got_w4.wait()
@@ -293,15 +315,20 @@
         z_send[n] = total.astype(BF).reshape(SIDE, 32, 512)
         z_own[n] = total.reshape(SIDE, 32, 512)
 
-    def input_rows(c):
-        ig[c] = tn(recv_d[c].reshape(512, tokens), w1r[...]).astype(BF)
-        at = pl.ds(pl.multiple_of(c * tokens, tokens), tokens)
-        pltpu.make_async_copy(ig.at[c], ig_hbm.at[at], store_sem.at[1, c]).start()
+    def stored(c, n):
+        at = pl.ds(c * tokens + n * piece, piece)
+        return pltpu.make_async_copy(ig.at[c, pl.ds(n * piece, piece)], ig_hbm.at[at], store_sem.at[1, c * PIECES + n])
+
+    def input_rows(c, pieces):
+        for n in pieces:
+            at = slice(n * piece, (n + 1) * piece)
+            ig[c, at] = tn(recv_d[c, :, :, at].reshape(512, piece), w1r[...]).astype(BF)
+            stored(c, n).start()
 
     def last_backward(c, _):
         arrived(3, c, recv_d)
         s1[...] += nn(recv_d[c].reshape(512, tokens), x[c])
-        input_rows(c)
+        input_rows(c, range(PIECES))
         return 0
 
     lax.fori_loop(0, CHUNKS - 1, last_backward, 0)
@@ -324,9 +351,10 @@
     parts = [tn(s1[:, j * 128 : (j + 1) * 128].astype(BF), pick_first(j)) for j in range(4)]
     y1_send[...] = own_rows(parts).reshape(4, 128, 128).astype(BF)
     scatter_y(4, y1_send, y1_recv)
-    input_rows(CHUNKS - 1)
+    input_rows(CHUNKS - 1, range(PIECES // 2))
     fold(4, y1_send, y1_recv, z1_send, z1_own)
     scatter_z(6, z1_send, z1_recv)
+    input_rows(CHUNKS - 1, range(PIECES // 2, PIECES))
 
     for n in range(2):
         wait_bytes(z_recv.at[n, pl.ds(0, SIDE - 1)], rs_recv.at[(2, 5)[n]])
@@ -349,7 +377,8 @@
     for c in range(CHUNKS):
         at = pl.ds(c * tokens, tokens)
         pltpu.make_async_copy(res.at[c], res_hbm.at[at], store_sem.at[0, c]).wait()
-        pltpu.make_async_copy(ig.at[c], ig_hbm.at[at], store_sem.at[1, c]).wait()
+        for n in range(PIECES):
+            stored(c, n).wait()
         for phase, send in enumerate((send_a, send_b, send_c, send_d)):
             wait_bytes(send.at[c, pl.ds(0, 15)], a2a_send.at[phase, c])
     wait_bytes(y_send.at[pl.ds(0, SIDE - 1)], rs_send.at[0])
@@ -424,7 +453,7 @@
             pltpu.VMEM((SIDE, 128, 128), BF), pltpu.VMEM((SIDE, 128, 128), BF),
             pltpu.VMEM((SIDE, 32, 128), BF), pltpu.VMEM((SIDE, 32, 128), BF),
             pltpu.VMEM((SIDE, 32, 128), F32),
-            pltpu.SemaphoreType.DMA((2 * CHUNKS + 4,)), pltpu.SemaphoreType.DMA((2, CHUNKS)),
+            pltpu.SemaphoreType.DMA((2 * CHUNKS + 3 + PIECES,)), pltpu.SemaphoreType.DMA((2, CHUNKS * PIECES)),
             pltpu.SemaphoreType.DMA((4, CHUNKS)), pltpu.SemaphoreType.DMA((4, CHUNKS)),
             pltpu.SemaphoreType.DMA((7,)), pltpu.SemaphoreType.DMA((7,)),
         ],

time: 117 us -> 116 us (level)
  no operation moved by 1% of the time
where the time goes in v4:
time: 116 us
  Pallas kernels  115 us (99%)
    pallas_call x1, Pallas kernels, local(): pl.pallas_call(kernel, out_shape=outs, in_specs=[any_spec] * 6, out_specs...  113 us
    pallas_call x1, Pallas kernels, local(): pl.pallas_call(publish, out_shape=outs, in_specs=[any_spec] * 6, out_spec...  2.68 us

profile of v4, /device:TPU:2, one launch (start us, length us, event | category | flops | bytes accessed | tf_op | source)
XLA Modules:
  0.0 115.9 jit_solution(922038237628567179)
XLA Ops:
  0.6 112.5 %shard_map.109 = (bf16[1024,512]{1,0:T(8,128)(2,1)}, bf16[1024,512]{1,0:T(8,128)(2,1)}, f32[4,8,128]{2,1,0:T(8,128)}, f32[4,8,512]{2,1,0:T(8,128)}, f32[4,32,128]{2,1,0:T(8,128)}, /*index=5*/f32[4,8,128]{2,1,0:T(8,128)}) custom-call(bf16[1024,512]{1,0:T(8,128)(2,1)} %x_hbm.1, bf16[1024,512]{1,0:T(8,128)(2,1)} %cot_hbm.1, bf16[4,128,128]{2,1,0:T(8,128)(2,1)} %w1_hbm.1, ...), custom_call_target="tpu_custom_call" | custom-call | flops 8000000000 | bytes 6000000 | tf_op jit(solution)/shard_map/pallas_call | solution.py:430
  113.2 2.7 %shard_map.110 = (bf16[1024,512]{1,0:T(8,128)(2,1)}, bf16[1024,512]{1,0:T(8,128)(2,1)}, f32[4,8,128]{2,1,0:T(8,128)}, f32[4,8,512]{2,1,0:T(8,128)}, f32[4,32,128]{2,1,0:T(8,128)}, /*index=5*/f32[4,8,128]{2,1,0:T(8,128)}) custom-call(bf16[1024,512]{1,0:T(8,128)(2,1)} %get-tuple-element.12.refs_0_, bf16[1024,512]{1,0:T(8,128)(2,1)} %get-tuple-element.13.refs_1_, ...), custom_call_target="tpu_custom_call" | custom-call | bytes 5000000 | tf_op jit(solution)/shard_map/pallas_call | solution.py:465

commit v5 on v4

--- a/solution.py
+++ b/solution.py
@@ -394,7 +394,7 @@
     sources, targets, held, sem = refs[:6], refs[6:12], refs[12:18], refs[18]
     copies = []
     for n, (source, target, slot) in enumerate(zip(sources, targets, held)):
-        parts = CHUNKS if n < 2 else 1
+        parts = PIECES if n < 2 else 1
         rows = source.shape[0] // parts
         for i in range(parts):
             at = pl.ds(i * rows, rows)
@@ -468,7 +468,7 @@
         in_specs=[any_spec] * 6,
         out_specs=(any_spec,) * 6,
         scratch_shapes=[pltpu.VMEM(out.shape, out.dtype) for out in outs]
-        + [pltpu.SemaphoreType.DMA((2, 2 * CHUNKS + 4))],
+        + [pltpu.SemaphoreType.DMA((2, 2 * PIECES + 4))],
         cost_estimate=pl.CostEstimate(flops=0, bytes_accessed=5 * 10**6, transcendentals=0),
     )(*made)
 

time: 116 us -> 116 us (level)
  no operation moved by 1% of the time
where the time goes in v5:
time: 116 us
  Pallas kernels  115 us (99%)
    pallas_call x1, Pallas kernels, local(): pl.pallas_call(kernel, out_shape=outs, in_specs=[any_spec] * 6, out_specs...  113 us
    pallas_call x1, Pallas kernels, local(): pl.pallas_call(publish, out_shape=outs, in_specs=[any_spec] * 6, out_spec...  2.51 us

profile of v5, /device:TPU:2, one launch (start us, length us, event | category | flops | bytes accessed | tf_op | source)
XLA Modules:
  0.0 115.7 jit_solution(14243604488156187172)
XLA Ops:
  0.6 112.5 %shard_map.109 = (bf16[1024,512]{1,0:T(8,128)(2,1)}, bf16[1024,512]{1,0:T(8,128)(2,1)}, f32[4,8,128]{2,1,0:T(8,128)}, f32[4,8,512]{2,1,0:T(8,128)}, f32[4,32,128]{2,1,0:T(8,128)}, /*index=5*/f32[4,8,128]{2,1,0:T(8,128)}) custom-call(bf16[1024,512]{1,0:T(8,128)(2,1)} %x_hbm.1, bf16[1024,512]{1,0:T(8,128)(2,1)} %cot_hbm.1, bf16[4,128,128]{2,1,0:T(8,128)(2,1)} %w1_hbm.1, ...), custom_call_target="tpu_custom_call" | custom-call | flops 8000000000 | bytes 6000000 | tf_op jit(solution)/shard_map/pallas_call | solution.py:430
  113.2 2.5 %shard_map.110 = (bf16[1024,512]{1,0:T(8,128)(2,1)}, bf16[1024,512]{1,0:T(8,128)(2,1)}, f32[4,8,128]{2,1,0:T(8,128)}, f32[4,8,512]{2,1,0:T(8,128)}, f32[4,32,128]{2,1,0:T(8,128)}, /*index=5*/f32[4,8,128]{2,1,0:T(8,128)}) custom-call(bf16[1024,512]{1,0:T(8,128)(2,1)} %get-tuple-element.12.refs_0_, bf16[1024,512]{1,0:T(8,128)(2,1)} %get-tuple-element.13.refs_1_, ...), custom_call_target="tpu_custom_call" | custom-call | bytes 5000000 | tf_op jit(solution)/shard_map/pallas_call | solution.py:465
